TPU v7x, 32 devices: a whole 2x2x4 slice. The times are simulated.
32 devices in a mesh: groups: 2 (over y), seq: 16 (over z, x, core).
Axes of the slice: x: 2, y: 2, z: 4, core: 2. Of those that a mesh axis runs over, the one named last changes fastest.
Arguments:
- query_in: bfloat16 [16384, 128], P(('groups', 'seq')), parts along dimension 0, may hold values from -6 to 6
- key_in: bfloat16 [16384, 128], P(('groups', 'seq')), parts along dimension 0, may hold values from -6 to 6
- value_in: bfloat16 [16384, 1024], P(('groups', 'seq')), parts along dimension 0, may hold values from -12 to 12
- conv_weight: float32 [3, 1024], replicated, may hold values from -3 to 3
- norm_gain: float32 [1024], replicated, may hold values from 0.1 to 1.9
- window_query: bfloat16 [16384, 1024], P(('groups', 'seq')), parts along dimension 0, may hold values from -6 to 6
- window_key: bfloat16 [16384, 1024], P(('groups', 'seq')), parts along dimension 0, may hold values from -6 to 6
- cotangent: bfloat16 [16384, 1024], P(('groups', 'seq')), parts along dimension 0, may hold values from -6 to 6
Outputs:
- layer_out: bfloat16 [16384, 1024], P(('groups', 'seq')), parts along dimension 0
- query_grad: bfloat16 [16384, 128], P(('groups', 'seq')), parts along dimension 0
- key_grad: bfloat16 [16384, 128], P(('groups', 'seq')), parts along dimension 0
- window_grad: bfloat16 [2, 16384, 1024], P(None, ('groups', 'seq')), parts along dimension 1
- value_grad: bfloat16 [16384, 1024], P(('groups', 'seq')), parts along dimension 0
There are 2 independent parts, one for each index of `groups`. A program takes and returns all parts, laid end to end along the dimension named above; an argument that names none is the same for every part. Nothing has to cross between parts.
All inputs are finite; a program needn't handle non-finite values.
Results may differ from a plain program's by a relative error of at most 0.0077.
Values may be sent and summed in bfloat16 or wider, within the bound.
A program may use at most 192 MiB of HBM per device.

v0:
```python
from functools import partial

import jax
import jax.numpy as jnp
import numpy as np
from jax import lax
from jax.experimental import pallas as pl
from jax.experimental.pallas import tpu as pltpu
from jax.sharding import PartitionSpec as P

H = 8
DK = 16
DV = 128
WIN = 64
KC = 3
FP = 160
RIM = WIN + 16
TAIL = 8
EPS = 1e-05
F32 = jnp.float32
BF16 = jnp.bfloat16


def feature_tables():
    e1 = np.zeros((FP, DK), np.float32)
    e2 = np.zeros((FP, DK), np.float32)
    b1 = np.zeros((FP,), np.float32)
    b2 = np.zeros((FP,), np.float32)
    w = np.zeros((FP,), np.float32)
    for i in range(DK):
        e1[i, i], b2[i], w[i] = 1, 1, 0.25
    for d in range(DK // 2 + 1):
        for i in range(DK if d < DK // 2 else DK // 2):
            f = DK + DK * d + i
            e1[f, i], e2[f, (i + d) % DK] = 1, 1
            w[f] = 1 / 32 if d == 0 else 1 / 16
    one = DK + DK * (DK // 2) + DK // 2
    b1[one], b2[one], w[one] = 1, 1, 1
    columns = np.repeat(np.stack([b1, b2, w])[:, :, None], 128, axis=2)
    rows = np.concatenate([np.stack([b1, b2, w]), np.zeros((5, FP), np.float32)])
    return np.tile(e1, (1, H)), np.tile(e2, (1, H)), columns, rows


def nn(a, b):
    return lax.dot_general(a, b, (((1,), (0,)), ((), ())), preferred_element_type=F32)


def nt(a, b):
    return lax.dot_general(a, b, (((1,), (1,)), ((), ())), preferred_element_type=F32)


def tn(a, b):
    return lax.dot_general(a, b, (((0,), (0,)), ((), ())), preferred_element_type=F32)


def split(x):
    high = x.astype(BF16)
    return high, (x - high.astype(F32)).astype(BF16)


def body(
    n, plane,
    q_ref, k_ref, v_ref, cw_ref, gain_ref, wq_ref, wk_ref, ct_ref, e1_ref, e2_ref, col_ref, row_ref,
    lo_ref, qg_ref, kg_ref, wg_ref, vg_ref,
    vrim, krim, kback_out, vback_out, kback, vback, vnext_out, vnext,
    cv, num, wo, kw, vw, ng, dq, dk,
    loc, buf_a, tot, buf_b, base, stage, buf_c,
    rim_s, rim_r, back_s, back_r, next_s, next_r, a_s, a_r, b_s, b_r, c_s, c_r,
):
    T = q_ref.shape[0]
    deep = n // plane
    own_heads = H // plane
    R = own_heads * FP
    HALF = T // 2
    me = lax.axis_index("seq")
    z = lax.div(me, plane)
    p = lax.rem(me, plane)

    def remote(src, dst, ss, rs, to):
        return pltpu.make_async_remote_copy(
            src_ref=src, dst_ref=dst, send_sem=ss, recv_sem=rs,
            device_id={"seq": to}, device_id_type=pl.DeviceIdType.MESH,
        )

    barrier = pltpu.get_barrier_semaphore()

    def greet(to):
        pl.semaphore_signal(barrier, inc=1, device_id={"seq": to}, device_id_type=pl.DeviceIdType.MESH)

    for r in range(1, plane):
        greet(z * plane + lax.rem(p + r, plane))
    for r in range(1, deep):
        greet(lax.rem(z + r, deep) * plane + p)
    pl.when(p == 0)(lambda: greet(lax.rem(me + n - 1, n)))
    pl.when(p == plane - 1)(lambda: greet(lax.rem(me + 1, n)))
    edge = jnp.where((p == 0) | (p == plane - 1), 1, 0)
    pl.semaphore_wait(barrier, plane - 1 + deep - 1 + edge)

    def rim_copies():
        return (
            remote(v_ref.at[pl.ds(T - RIM, RIM)], vrim, rim_s.at[0], rim_r.at[0], me + 1),
            remote(wk_ref.at[pl.ds(T - WIN, WIN)], krim, rim_s.at[1], rim_r.at[1], me + 1),
        )

    def back_copies():
        return (
            remote(kback_out, kback, back_s.at[0], back_r.at[0], me - 1),
            remote(vback_out, vback, back_s.at[1], back_r.at[1], me - 1),
        )

    def next_copy():
        return (remote(vnext_out, vnext, next_s.at[0], next_r.at[0], me - 1),)

    def begin(copies):
        for c in copies:
            c.start()

    def arrived(copies):
        for c in copies:
            c.wait_recv()

    def sent(copies):
        for c in copies:
            c.wait_send()

    def copies_a(i):
        out = []
        for r in range(1, plane):
            to = lax.rem(p + r, plane)
            out.append(remote(
                loc.at[i, pl.ds(pl.multiple_of(to * R, 16), R)], buf_a.at[i, r],
                a_s.at[i, r], a_r.at[i, r], z * plane + to))
        return out

    def copies_b(i):
        out = []
        for r in range(1, deep):
            to = z + r if i == 0 else z - r
            ok = to < deep if i == 0 else to >= 0
            source = z - r if i == 0 else z + r
            comes = source >= 0 if i == 0 else source < deep
            out.append((ok, comes, r, remote(
                tot.at[i], buf_b.at[i, r], b_s.at[i, r], b_r.at[i, r], to * plane + p)))
        return out

    def copies_c(i):
        out = []
        for r in range(1, plane):
            to = lax.rem(p + r, plane)
            out.append(remote(
                stage.at[i, to], buf_c.at[i, r], c_s.at[i, r], c_r.at[i, r], z * plane + to))
        return out

    def scan_a(i):
        begin(copies_a(i))
        buf_a[i, 0] = loc[i, pl.ds(pl.multiple_of(p * R, 16), R)]

    def scan_b(i):
        arrived(copies_a(i))
        total = buf_a[i, 0].astype(F32)
        for r in range(1, plane):
            total = total + buf_a[i, r].astype(F32)
        tot[i] = total.astype(BF16)
        for ok, _, _, c in copies_b(i):
            pl.when(ok)(c.start)

    def scan_c(i):
        base[...] = jnp.zeros_like(base)
        for _, comes, r, c in copies_b(i):
            @pl.when(comes)
            def _():
                c.wait_recv()
                base[...] += buf_b[i, r].astype(F32)
        running = base[...]
        order = range(plane) if i == 0 else range(plane - 1, -1, -1)
        for d in order:
            stage[i, d] = running.astype(BF16)
            running = running + buf_a[i, lax.rem(p - d + plane, plane)].astype(F32)
        begin(copies_c(i))
        buf_c[i, 0] = stage[i, p]

    def scan_end(i):
        arrived(copies_c(i))

    def scan_sent(i):
        sent(copies_a(i))
        for ok, _, _, c in copies_b(i):
            pl.when(ok)(c.wait_send)
        sent(copies_c(i))

    def prior(i, h):
        slot = lax.rem(p - lax.div(h, own_heads) + plane, plane)
        at = pl.multiple_of(lax.rem(h, own_heads) * FP, 16)
        return (buf_c[i, slot, pl.ds(at, FP), :].astype(F32) * col_ref[2]).astype(BF16)

    def cols(h):
        return pl.ds(pl.multiple_of(h * DV, DV), DV)

    def of_head(h, rows):
        return lax.div(lax.broadcasted_iota(jnp.int32, (rows, 128), 1), DK) == h

    def masked(h, x):
        return jnp.where(of_head(h, x.shape[0]), x, jnp.zeros_like(x))

    def factors(x):
        return nt(x, e1_ref[...]) + row_ref[0:1], nt(x, e2_ref[...]) + row_ref[1:2]

    def turned(x):
        return (nt(e1_ref[...], x) + col_ref[0, :, 0:1]) * (nt(e2_ref[...], x) + col_ref[1, :, 0:1])

    def heads(low, high, f):
        def step(h, carry):
            f(h)
            return carry
        lax.fori_loop(low, high, step, 0)

    pl.when(me < n - 1)(lambda: begin(rim_copies()))

    @pl.when(me == 0)
    def _():
        vrim[...] = jnp.zeros_like(vrim)
        krim[...] = jnp.zeros_like(krim)

    pl.when(me > 0)(lambda: arrived(rim_copies()))

    def conv_state(h):
        at = cols(h)
        ext = jnp.concatenate([vrim[:, at].astype(F32), v_ref[:, at].astype(F32)], axis=0)
        mixed = (
            cw_ref[0:1, at] * ext
            + cw_ref[1:2, at] * pltpu.roll(ext, 1, 0)
            + cw_ref[2:3, at] * pltpu.roll(ext, 2, 0)
        )[RIM - WIN :].astype(BF16)
        cv[:, at] = mixed
        high, low = split(turned(masked(h, k_ref[...])))
        own = mixed[WIN:]
        loc[0, pl.ds(pl.multiple_of(h * FP, 16), FP), :] = (nn(high, own) + nn(low, own)).astype(BF16)

    heads(0, H, conv_state)
    scan_a(0)

    QB = 128
    KB = QB + WIN
    not_first = me > 0

    def window(h):
        at = cols(h)
        kw[:, at] = jnp.zeros((T + WIN, DV), F32)
        vw[:, at] = jnp.zeros((T + WIN, DV), F32)
        t_at = lax.broadcasted_iota(jnp.int32, (QB, KB), 0)
        s_at = lax.broadcasted_iota(jnp.int32, (QB, KB), 1)
        band = (s_at > t_at) & (s_at <= t_at + WIN)
        for b in range(T // QB):
            rows = pl.ds(b * QB, QB)
            span = pl.ds(b * QB, KB)
            if b == 0:
                keys = jnp.concatenate([krim[:, at], wk_ref[0:QB, at]], axis=0)
                allowed = band & ((s_at >= WIN) | not_first)
            else:
                keys = wk_ref[pl.ds(b * QB - WIN, KB), at]
                allowed = band
            queries = wq_ref[rows, at]
            values = cv[span, at]
            grads = ct_ref[rows, at]
            scores = jnp.where(allowed, nt(queries, keys) * DV ** (-0.5), -jnp.inf)
            power = jnp.exp(scores - jnp.max(scores, axis=1, keepdims=True))
            attention = power / jnp.sum(power, axis=1, keepdims=True)
            low = attention.astype(BF16)
            wo[rows, at] = nn(low, values)
            grad = nt(grads, values)
            change = attention * (grad - jnp.sum(attention * grad, axis=1, keepdims=True))
            change = (change * DV ** (-0.5)).astype(BF16)
            wg_ref[0, rows, at] = nn(change, keys).astype(BF16)
            kw[span, at] += tn(change, queries)
            vw[span, at] += tn(low, grads)
        kback_out[:, at] = kw[0:WIN, at].astype(BF16)
        vback_out[:, at] = vw[0:WIN, at].astype(BF16)

    def causal(r, width):
        t_at = lax.broadcasted_iota(jnp.int32, (HALF, width), 0) + r * HALF
        return lax.broadcasted_iota(jnp.int32, (HALF, width), 1) <= t_at

    def near(h):
        at = cols(h)
        queries = masked(h, q_ref[...])
        for r in range(2):
            width = (r + 1) * HALF
            s = nt(queries[r * HALF : (r + 1) * HALF], k_ref[0:width]) * 0.25
            kernel = jnp.where(causal(r, width), 1.0 + s + 0.5 * s * s, 0.0).astype(BF16)
            num[pl.ds(r * HALF, HALF), at] = nn(kernel, cv[pl.ds(WIN, width), at])

    heads(0, 3, window)
    scan_b(0)
    heads(3, H, window)
    scan_c(0)
    pl.when(me > 0)(lambda: begin(back_copies()))
    heads(0, H, near)
    scan_end(0)

    def normed(h):
        at = cols(h)
        state = prior(0, h)
        queries = masked(h, q_ref[...])
        one, two = factors(queries)
        high, low = split(one * two)
        top = num[:, at] + nn(high, state) + nn(low, state)
        gain = gain_ref[0:1, at]
        scale = lax.rsqrt(jnp.mean(top * top, axis=1, keepdims=True) + EPS)
        lo_ref[:, at] = (gain * top * scale + wo[:, at]).astype(BF16)
        wanted = ct_ref[:, at].astype(F32) * gain
        pull = scale * wanted - top * (scale * scale * scale) * jnp.mean(wanted * top, axis=1, keepdims=True)
        pull = pull.astype(BF16)
        ng[:, at] = pull
        high, low = split(turned(queries))
        loc[1, pl.ds(pl.multiple_of(h * FP, 16), FP), :] = (nn(high, pull) + nn(low, pull)).astype(BF16)

    heads(0, H, normed)
    scan_a(1)
    dq[...] = jnp.zeros_like(dq)
    dk[...] = jnp.zeros_like(dk)

    def through(h, change, x):
        one, two = factors(x)
        out = nn((change * two).astype(BF16), e1_ref[...]) + nn((change * one).astype(BF16), e2_ref[...])
        return masked(h, out)

    def near_back(h):
        at = cols(h)
        queries = masked(h, q_ref[...])
        keys = masked(h, k_ref[...])
        for r in range(2):
            width = (r + 1) * HALF
            rows = pl.ds(r * HALF, HALF)
            mine = queries[r * HALF : (r + 1) * HALF]
            allowed = causal(r, width)
            s = nt(mine, keys[0:width]) * 0.25
            kernel = jnp.where(allowed, 1.0 + s + 0.5 * s * s, 0.0).astype(BF16)
            pull = ng[rows, at]
            change = jnp.where(allowed, nt(pull, cv[pl.ds(WIN, width), at]) * (0.25 + 0.25 * s), 0.0)
            change = change.astype(BF16)
            dq[rows, :] += nn(change, keys[0:width])
            dk[0:width, :] += tn(change, mine)
            vw[pl.ds(WIN, width), at] += tn(kernel, pull)
        dq[...] += through(h, nt(ng[:, at], prior(0, h)), queries)

    heads(0, 3, near_back)
    scan_b(1)
    heads(3, 6, near_back)
    scan_c(1)
    heads(6, H, near_back)
    qg_ref[...] = dq[...].astype(BF16)

    @pl.when(me < n - 1)
    def _():
        arrived(back_copies())
        kw[pl.ds(T, WIN), :] += kback[...].astype(F32)
        vw[pl.ds(T, WIN), :] += vback[...].astype(F32)

    wg_ref[1] = kw[pl.ds(WIN, T), :].astype(BF16)
    scan_end(1)

    def far_value(h):
        at = cols(h)
        one, two = factors(masked(h, k_ref[...]))
        high, low = split(one * two)
        state = prior(1, h)
        vw[pl.ds(WIN, T), at] += nn(high, state) + nn(low, state)
        vnext_out[:, at] = vw[pl.ds(WIN, TAIL), at]

    heads(0, H, far_value)
    pl.when(me > 0)(lambda: begin(next_copy()))

    def far_key(h):
        at = cols(h)
        dk[...] += through(h, nt(cv[pl.ds(WIN, T), at], prior(1, h)), masked(h, k_ref[...]))

    heads(0, H, far_key)
    kg_ref[...] = dk[...].astype(BF16)

    @pl.when(me == n - 1)
    def _():
        vnext[...] = jnp.zeros_like(vnext)

    pl.when(me < n - 1)(lambda: arrived(next_copy()))

    def conv_back(h):
        at = cols(h)
        ext = jnp.concatenate([vw[pl.ds(WIN, T), at], vnext[:, at]], axis=0)
        mixed = (
            cw_ref[0:1, at] * ext
            + cw_ref[1:2, at] * pltpu.roll(ext, T + TAIL - 1, 0)
            + cw_ref[2:3, at] * pltpu.roll(ext, T + TAIL - 2, 0)
        )
        vg_ref[:, at] = mixed[0:T].astype(BF16)

    heads(0, H, conv_back)

    pl.when(me < n - 1)(lambda: sent(rim_copies()))
    pl.when(me > 0)(lambda: sent(back_copies()))
    pl.when(me > 0)(lambda: sent(next_copy()))
    scan_sent(0)
    scan_sent(1)


def shards(n, query_in, key_in, value_in, conv_weight, norm_gain, window_query, window_key, cotangent):
    T, width = value_in.shape
    plane = min(H, 1 << ((n.bit_length() - 1) // 2))
    deep = n // plane
    R = H // plane * FP
    e1, e2, columns, rows = feature_tables()
    vmem = pl.BlockSpec(memory_space=pltpu.VMEM)
    dma = pltpu.SemaphoreType.DMA
    return pl.pallas_call(
        partial(body, n, plane),
        out_shape=(
            jax.ShapeDtypeStruct((T, width), BF16),
            jax.ShapeDtypeStruct((T, H * DK), BF16),
            jax.ShapeDtypeStruct((T, H * DK), BF16),
            jax.ShapeDtypeStruct((2, T, width), BF16),
            jax.ShapeDtypeStruct((T, width), BF16),
        ),
        in_specs=[vmem] * 12,
        out_specs=(vmem,) * 5,
        scratch_shapes=[
            pltpu.VMEM((RIM, width), BF16),
            pltpu.VMEM((WIN, width), BF16),
            pltpu.VMEM((WIN, width), BF16),
            pltpu.VMEM((WIN, width), BF16),
            pltpu.VMEM((WIN, width), BF16),
            pltpu.VMEM((WIN, width), BF16),
            pltpu.VMEM((TAIL, width), F32),
            pltpu.VMEM((TAIL, width), F32),
            pltpu.VMEM((T + WIN, width), BF16),
            pltpu.VMEM((T, width), F32),
            pltpu.VMEM((T, width), F32),
            pltpu.VMEM((T + WIN, width), F32),
            pltpu.VMEM((T + WIN, width), F32),
            pltpu.VMEM((T, width), BF16),
            pltpu.VMEM((T, H * DK), F32),
            pltpu.VMEM((T, H * DK), F32),
            pltpu.VMEM((2, H * FP, DV), BF16),
            pltpu.VMEM((2, plane, R, DV), BF16),
            pltpu.VMEM((2, R, DV), BF16),
            pltpu.VMEM((2, deep, R, DV), BF16),
            pltpu.VMEM((R, DV), F32),
            pltpu.VMEM((2, plane, R, DV), BF16),
            pltpu.VMEM((2, plane, R, DV), BF16),
            dma((2,)), dma((2,)), dma((2,)), dma((2,)), dma((1,)), dma((1,)),
            dma((2, plane)), dma((2, plane)), dma((2, deep)), dma((2, deep)),
            dma((2, plane)), dma((2, plane)),
        ],
        compiler_params=pltpu.CompilerParams(
            collective_id=0, has_side_effects=True, vmem_limit_bytes=56 * 1024 * 1024
        ),
    )(
        query_in, key_in, value_in, conv_weight, norm_gain.reshape(1, width), window_query, window_key,
        cotangent, jnp.asarray(e1, BF16), jnp.asarray(e2, BF16), jnp.asarray(columns), jnp.asarray(rows),
    )


def solution(mesh):
    tokens = P(("groups", "seq"), None)
    in_specs = (tokens, tokens, tokens, P(), P(), tokens, tokens, tokens)
    out_specs = (tokens, tokens, tokens, P(None, ("groups", "seq"), None), tokens)
    return jax.shard_map(
        partial(shards, mesh.shape["seq"]), mesh=mesh, in_specs=in_specs, out_specs=out_specs, check_vma=False
    )
```

profile of v0, /device:TPU:1, one launch (start us, length us, event | category | flops | bytes accessed | tf_op | source)
XLA Modules:
  0.0 91.4 jit_solution(4824623945115993113)
XLA Ops:
  0.6 83.1 %shard_map.155 = (bf16[512,1024]{1,0:T(8,128)(2,1)}, bf16[512,128]{1,0:T(8,128)(2,1)}, bf16[512,128]{1,0:T(8,128)(2,1)}, bf16[2,512,1024]{2,1,0:T(8,128)(2,1)}, bf16[512,1024]{1,0:T(8,128)(2,1)}) custom-call(bf16[512,128]{1,0:T(8,128)(2,1)} %q_ref.1, bf16[512,128]{1,0:T(8,128)(2,1)} %k_ref.1, bf16[512,1024]{1,0:T(8,128)(2,1)} %v_ref.1, f32[3,1024]{1,0:T(4,128)} %cw_ref.1, ...), custom_call_target="tpu_custom_call" | custom-call | tf_op jit(solution)/shard_map/pallas_call | solution.py:413
  83.8 0.0 copy-start.2
  83.8 0.0 copy-start
  83.8 2.4 %copy.22 = bf16[512,1024]{1,0:T(8,128)(2,1)} copy(bf16[512,1024]{1,0:T(8,128)(2,1)} %get-tuple-element.10) | data formatting | bytes 2097152
  86.2 1.6 %copy.23 = bf16[512,128]{1,0:T(8,128)(2,1)} copy(bf16[512,128]{1,0:T(8,128)(2,1)} %get-tuple-element.11) | data formatting | bytes 262144
  87.8 0.0 copy-done.2
  87.8 0.7 copy.24
  88.4 0.0 copy-done
  88.4 0.0 copy-start.1
  88.4 1.3 %copy.25 = bf16[2,512,1024]{2,1,0:T(8,128)(2,1)} copy(bf16[2,512,1024]{2,1,0:T(8,128)(2,1)S(1)} %copy-done) | data formatting | bytes 4194304
  89.7 0.6 copy-done.1
  90.4 1.0 %copy.26 = bf16[512,1024]{1,0:T(8,128)(2,1)} copy(bf16[512,1024]{1,0:T(8,128)(2,1)S(1)} %copy-done.1) | data formatting | bytes 2097152
Async XLA Ops:
  83.8 4.0 %copy-start.2 = (bf16[512,128]{1,0:T(8,128)(2,1)S(1)}, bf16[512,128]{1,0:T(8,128)(2,1)}, u32[]{:S(2)}) copy-start(bf16[512,128]{1,0:T(8,128)(2,1)} %get-tuple-element.12) | copy-start | bytes 393220
  83.8 4.7 %copy-start = (bf16[2,512,1024]{2,1,0:T(8,128)(2,1)S(1)}, bf16[2,512,1024]{2,1,0:T(8,128)(2,1)}, u32[]{:S(2)}) copy-start(bf16[2,512,1024]{2,1,0:T(8,128)(2,1)} %get-tuple-element.13) | copy-start | bytes 6291460
  88.4 2.0 %copy-start.1 = (bf16[512,1024]{1,0:T(8,128)(2,1)S(1)}, bf16[512,1024]{1,0:T(8,128)(2,1)}, u32[]{:S(2)}) copy-start(bf16[512,1024]{1,0:T(8,128)(2,1)} %get-tuple-element.14) | copy-start | bytes 3145732
where the time goes:
time: 91.6 us; the launch traced here: 91.4 us
  Pallas kernels  83.1 us (91%)
  local copies, waits for them, and re-layouts  7.57 us (8%)
    pallas_call x1, Pallas kernels, shards(): pl.pallas_call(partial(body, n, plane), out_shape=(jax.ShapeDtypeStruct((...  83.1 us
    unnamed x11, local copies, waits for them, and re-layouts  7.57 us

commit v1 on v0

--- a/solution.py
+++ b/solution.py
@@ -53,17 +53,12 @@
     return lax.dot_general(a, b, (((0,), (0,)), ((), ())), preferred_element_type=F32)
 
 
-def split(x):
-    high = x.astype(BF16)
-    return high, (x - high.astype(F32)).astype(BF16)
-
-
 def body(
     n, plane,
     q_ref, k_ref, v_ref, cw_ref, gain_ref, wq_ref, wk_ref, ct_ref, e1_ref, e2_ref, col_ref, row_ref,
     lo_ref, qg_ref, kg_ref, wg_ref, vg_ref,
     vrim, krim, kback_out, vback_out, kback, vback, vnext_out, vnext,
-    cv, num, wo, kw, vw, ng, dq, dk,
+    cv, num, wo, klast, vw, ng, dq, dk, pkt, pqt, pq, pk, qa, qb, ka, kb,
     loc, buf_a, tot, buf_b, base, stage, buf_c,
     rim_s, rim_r, back_s, back_r, next_s, next_r, a_s, a_r, b_s, b_r, c_s, c_r,
 ):
@@ -221,6 +216,10 @@
         vrim[...] = jnp.zeros_like(vrim)
         krim[...] = jnp.zeros_like(krim)
 
+    def key_features(h):
+        pkt[h] = turned(masked(h, k_ref[...])).astype(BF16)
+
+    heads(0, H, key_features)
     pl.when(me > 0)(lambda: arrived(rim_copies()))
 
     def conv_state(h):
@@ -232,9 +231,7 @@
             + cw_ref[2:3, at] * pltpu.roll(ext, 2, 0)
         )[RIM - WIN :].astype(BF16)
         cv[:, at] = mixed
-        high, low = split(turned(masked(h, k_ref[...])))
-        own = mixed[WIN:]
-        loc[0, pl.ds(pl.multiple_of(h * FP, 16), FP), :] = (nn(high, own) + nn(low, own)).astype(BF16)
+        loc[0, pl.ds(pl.multiple_of(h * FP, 16), FP), :] = nn(pkt[h], mixed[WIN:]).astype(BF16)
 
     heads(0, H, conv_state)
     scan_a(0)
@@ -245,36 +242,46 @@
 
     def window(h):
         at = cols(h)
-        kw[:, at] = jnp.zeros((T + WIN, DV), F32)
-        vw[:, at] = jnp.zeros((T + WIN, DV), F32)
-        t_at = lax.broadcasted_iota(jnp.int32, (QB, KB), 0)
-        s_at = lax.broadcasted_iota(jnp.int32, (QB, KB), 1)
+        s_at = lax.broadcasted_iota(jnp.int32, (KB, QB), 0)
+        t_at = lax.broadcasted_iota(jnp.int32, (KB, QB), 1)
         band = (s_at > t_at) & (s_at <= t_at + WIN)
-        for b in range(T // QB):
-            rows = pl.ds(b * QB, QB)
-            span = pl.ds(b * QB, KB)
-            if b == 0:
-                keys = jnp.concatenate([krim[:, at], wk_ref[0:QB, at]], axis=0)
-                allowed = band & ((s_at >= WIN) | not_first)
+        blocks = range(T // QB)
+        spans = [pl.ds(b * QB, KB) for b in blocks]
+        rows = [pl.ds(b * QB, QB) for b in blocks]
+        keys = [
+            wk_ref[pl.ds(b * QB - WIN, KB), at] if b
+            else jnp.concatenate([krim[:, at], wk_ref[0:QB, at]], axis=0)
+            for b in blocks
+        ]
+        scores = [nt(keys[b], wq_ref[rows[b], at]) for b in blocks]
+        grad = [nt(cv[spans[b], at], ct_ref[rows[b], at]) for b in blocks]
+        low, change = [], []
+        for b in blocks:
+            allowed = band if b else band & ((s_at >= WIN) | not_first)
+            masked_scores = jnp.where(allowed, scores[b] * DV ** (-0.5), -jnp.inf)
+            power = jnp.exp(masked_scores - jnp.max(masked_scores, axis=0, keepdims=True))
+            attention = power * (1.0 / jnp.sum(power, axis=0, keepdims=True))
+            low.append(attention.astype(BF16))
+            mean = jnp.sum(attention * grad[b], axis=0, keepdims=True)
+            change.append((attention * (grad[b] - mean) * DV ** (-0.5)).astype(BF16))
+        key_parts = [nn(change[b], wq_ref[rows[b], at]) for b in blocks]
+        value_parts = [nn(low[b], ct_ref[rows[b], at]) for b in blocks]
+        for b in blocks:
+            wo[rows[b], at] = tn(low[b], cv[spans[b], at])
+            wg_ref[0, rows[b], at] = tn(change[b], keys[b]).astype(BF16)
+        kback_out[:, at] = key_parts[0][0:WIN].astype(BF16)
+        vback_out[:, at] = value_parts[0][0:WIN].astype(BF16)
+        for b in blocks:
+            mid = pl.ds(b * QB, WIN)
+            wg_ref[1, mid, at] = key_parts[b][WIN:QB].astype(BF16)
+            vw[mid, at] = value_parts[b][WIN:QB]
+            end = pl.ds(b * QB + WIN, WIN)
+            if b < T // QB - 1:
+                wg_ref[1, end, at] = (key_parts[b][QB:] + key_parts[b + 1][0:WIN]).astype(BF16)
+                vw[end, at] = value_parts[b][QB:] + value_parts[b + 1][0:WIN]
             else:
-                keys = wk_ref[pl.ds(b * QB - WIN, KB), at]
-                allowed = band
-            queries = wq_ref[rows, at]
-            values = cv[span, at]
-            grads = ct_ref[rows, at]
-            scores = jnp.where(allowed, nt(queries, keys) * DV ** (-0.5), -jnp.inf)
-            power = jnp.exp(scores - jnp.max(scores, axis=1, keepdims=True))
-            attention = power / jnp.sum(power, axis=1, keepdims=True)
-            low = attention.astype(BF16)
-            wo[rows, at] = nn(low, values)
-            grad = nt(grads, values)
-            change = attention * (grad - jnp.sum(attention * grad, axis=1, keepdims=True))
-            change = (change * DV ** (-0.5)).astype(BF16)
-            wg_ref[0, rows, at] = nn(change, keys).astype(BF16)
-            kw[span, at] += tn(change, queries)
-            vw[span, at] += tn(low, grads)
-        kback_out[:, at] = kw[0:WIN, at].astype(BF16)
-        vback_out[:, at] = vw[0:WIN, at].astype(BF16)
+                klast[:, at] = key_parts[b][QB:]
+                vw[end, at] = value_parts[b][QB:]
 
     def causal(r, width):
         t_at = lax.broadcasted_iota(jnp.int32, (HALF, width), 0) + r * HALF
@@ -288,22 +295,25 @@
             s = nt(queries[r * HALF : (r + 1) * HALF], k_ref[0:width]) * 0.25
             kernel = jnp.where(causal(r, width), 1.0 + s + 0.5 * s * s, 0.0).astype(BF16)
             num[pl.ds(r * HALF, HALF), at] = nn(kernel, cv[pl.ds(WIN, width), at])
+        one, two = factors(queries)
+        qa[h] = one.astype(BF16)
+        qb[h] = two.astype(BF16)
+        pq[h] = (one * two).astype(BF16)
+        pqt[h] = turned(queries).astype(BF16)
 
     heads(0, 3, window)
     scan_b(0)
     heads(3, H, window)
+    pl.when(me > 0)(lambda: begin(back_copies()))
+    heads(0, 2, near)
     scan_c(0)
-    pl.when(me > 0)(lambda: begin(back_copies()))
-    heads(0, H, near)
+    heads(2, H, near)
     scan_end(0)
 
     def normed(h):
         at = cols(h)
         state = prior(0, h)
-        queries = masked(h, q_ref[...])
-        one, two = factors(queries)
-        high, low = split(one * two)
-        top = num[:, at] + nn(high, state) + nn(low, state)
+        top = num[:, at] + nn(pq[h], state)
         gain = gain_ref[0:1, at]
         scale = lax.rsqrt(jnp.mean(top * top, axis=1, keepdims=True) + EPS)
         lo_ref[:, at] = (gain * top * scale + wo[:, at]).astype(BF16)
@@ -311,17 +321,16 @@
         pull = scale * wanted - top * (scale * scale * scale) * jnp.mean(wanted * top, axis=1, keepdims=True)
         pull = pull.astype(BF16)
         ng[:, at] = pull
-        high, low = split(turned(queries))
-        loc[1, pl.ds(pl.multiple_of(h * FP, 16), FP), :] = (nn(high, pull) + nn(low, pull)).astype(BF16)
+        loc[1, pl.ds(pl.multiple_of(h * FP, 16), FP), :] = nn(pqt[h], pull).astype(BF16)
 
     heads(0, H, normed)
     scan_a(1)
     dq[...] = jnp.zeros_like(dq)
     dk[...] = jnp.zeros_like(dk)
 
-    def through(h, change, x):
-        one, two = factors(x)
-        out = nn((change * two).astype(BF16), e1_ref[...]) + nn((change * one).astype(BF16), e2_ref[...])
+    def through(h, change, one, two):
+        out = nn((change * two.astype(F32)).astype(BF16), e1_ref[...])
+        out = out + nn((change * one.astype(F32)).astype(BF16), e2_ref[...])
         return masked(h, out)
 
     def near_back(h):
@@ -340,39 +349,42 @@
             change = change.astype(BF16)
             dq[rows, :] += nn(change, keys[0:width])
             dk[0:width, :] += tn(change, mine)
-            vw[pl.ds(WIN, width), at] += tn(kernel, pull)
-        dq[...] += through(h, nt(ng[:, at], prior(0, h)), queries)
+            vw[pl.ds(0, width), at] += tn(kernel, pull)
+        dq[...] += through(h, nt(ng[:, at], prior(0, h)), qa[h], qb[h])
+
+    def key_factors(h):
+        one, two = factors(masked(h, k_ref[...]))
+        ka[h] = one.astype(BF16)
+        kb[h] = two.astype(BF16)
+        pk[h] = (one * two).astype(BF16)
 
     heads(0, 3, near_back)
     scan_b(1)
-    heads(3, 6, near_back)
+    heads(3, H, near_back)
     scan_c(1)
-    heads(6, H, near_back)
+    heads(0, H, key_factors)
     qg_ref[...] = dq[...].astype(BF16)
 
     @pl.when(me < n - 1)
     def _():
         arrived(back_copies())
-        kw[pl.ds(T, WIN), :] += kback[...].astype(F32)
-        vw[pl.ds(T, WIN), :] += vback[...].astype(F32)
-
-    wg_ref[1] = kw[pl.ds(WIN, T), :].astype(BF16)
+        klast[...] += kback[...].astype(F32)
+        vw[pl.ds(T - WIN, WIN), :] += vback[...].astype(F32)
+
+    wg_ref[1, pl.ds(T - WIN, WIN), :] = klast[...].astype(BF16)
     scan_end(1)
 
     def far_value(h):
         at = cols(h)
-        one, two = factors(masked(h, k_ref[...]))
-        high, low = split(one * two)
-        state = prior(1, h)
-        vw[pl.ds(WIN, T), at] += nn(high, state) + nn(low, state)
-        vnext_out[:, at] = vw[pl.ds(WIN, TAIL), at]
+        vw[:, at] += nn(pk[h], prior(1, h))
+        vnext_out[:, at] = vw[0:TAIL, at]
 
     heads(0, H, far_value)
     pl.when(me > 0)(lambda: begin(next_copy()))
 
     def far_key(h):
         at = cols(h)
-        dk[...] += through(h, nt(cv[pl.ds(WIN, T), at], prior(1, h)), masked(h, k_ref[...]))
+        dk[...] += through(h, nt(cv[pl.ds(WIN, T), at], prior(1, h)), ka[h], kb[h])
 
     heads(0, H, far_key)
     kg_ref[...] = dk[...].astype(BF16)
@@ -385,7 +397,7 @@
 
     def conv_back(h):
         at = cols(h)
-        ext = jnp.concatenate([vw[pl.ds(WIN, T), at], vnext[:, at]], axis=0)
+        ext = jnp.concatenate([vw[:, at], vnext[:, at]], axis=0)
         mixed = (
             cw_ref[0:1, at] * ext
             + cw_ref[1:2, at] * pltpu.roll(ext, T + TAIL - 1, 0)
@@ -400,6 +412,30 @@
     pl.when(me > 0)(lambda: sent(next_copy()))
     scan_sent(0)
     scan_sent(1)
+
+
+def copies(*refs):
+    count = len(refs) // 2
+    for i in range(count):
+        refs[count + i][...] = refs[i][...]
+
+
+def handed_on(arrays):
+    steps = 4
+
+    def block(a):
+        lead = a.ndim - 2
+        return pl.BlockSpec(
+            (*a.shape[:lead], a.shape[lead] // steps, a.shape[-1]), lambda i: (0,) * lead + (i, 0)
+        )
+
+    return pl.pallas_call(
+        copies,
+        grid=(steps,),
+        out_shape=tuple(jax.ShapeDtypeStruct(a.shape, a.dtype) for a in arrays),
+        in_specs=[block(a) for a in arrays],
+        out_specs=tuple(block(a) for a in arrays),
+    )(*arrays)
 
 
 def shards(n, query_in, key_in, value_in, conv_weight, norm_gain, window_query, window_key, cotangent):
@@ -410,7 +446,7 @@
     e1, e2, columns, rows = feature_tables()
     vmem = pl.BlockSpec(memory_space=pltpu.VMEM)
     dma = pltpu.SemaphoreType.DMA
-    return pl.pallas_call(
+    outs = pl.pallas_call(
         partial(body, n, plane),
         out_shape=(
             jax.ShapeDtypeStruct((T, width), BF16),
@@ -433,11 +469,14 @@
             pltpu.VMEM((T + WIN, width), BF16),
             pltpu.VMEM((T, width), F32),
             pltpu.VMEM((T, width), F32),
-            pltpu.VMEM((T + WIN, width), F32),
-            pltpu.VMEM((T + WIN, width), F32),
+            pltpu.VMEM((WIN, width), F32),
+            pltpu.VMEM((T, width), F32),
             pltpu.VMEM((T, width), BF16),
             pltpu.VMEM((T, H * DK), F32),
             pltpu.VMEM((T, H * DK), F32),
+            pltpu.VMEM((H, FP, T), BF16),
+            pltpu.VMEM((H, FP, T), BF16),
+            *[pltpu.VMEM((H, T, FP), BF16)] * 6,
             pltpu.VMEM((2, H * FP, DV), BF16),
             pltpu.VMEM((2, plane, R, DV), BF16),
             pltpu.VMEM((2, R, DV), BF16),
@@ -456,6 +495,7 @@
         query_in, key_in, value_in, conv_weight, norm_gain.reshape(1, width), window_query, window_key,
         cotangent, jnp.asarray(e1, BF16), jnp.asarray(e2, BF16), jnp.asarray(columns), jnp.asarray(rows),
     )
+    return handed_on(outs)
 
 
 def solution(mesh):

time: 91.6 us -> 70.5 us (0.77)
  Pallas kernels: 83.1 us -> 69.7 us
  local copies, waits for them, and re-layouts: 7.57 us -> 0 us
    pallas_call x1, Pallas kernels: 83.1 us -> 64.9 us  [shards(): pl.pallas_call(partial(body, n, plane), out_shape=(jax.ShapeDtypeStruct((...]
    unnamed x11 -> x0, local copies, waits for them, and re-layouts: 7.57 us -> none
    pallas_call x0 -> x1, Pallas kernels: none -> 4.82 us  [handed_on(): pl.pallas_call(copies, grid=(steps,), out_shape=tuple((jax.ShapeDtypeStru...]
where the time goes in v1:
time: 70.5 us; the launch traced here: 70.3 us
  Pallas kernels  69.7 us (99%)
    pallas_call x1, Pallas kernels, shards(): pl.pallas_call(partial(body, n, plane), out_shape=(jax.ShapeDtypeStruct((...  64.9 us
    pallas_call x1, Pallas kernels, handed_on(): pl.pallas_call(copies, grid=(steps,), out_shape=tuple((jax.ShapeDtypeStru...  4.82 us

profile of v1, /device:TPU:1, one launch (start us, length us, event | category | flops | bytes accessed | tf_op | source)
XLA Modules:
  0.0 70.3 jit_solution(2720016491215548413)
XLA Ops:
  0.6 64.9 %shard_map.155 = (bf16[512,1024]{1,0:T(8,128)(2,1)}, bf16[512,128]{1,0:T(8,128)(2,1)}, bf16[512,128]{1,0:T(8,128)(2,1)}, bf16[2,512,1024]{2,1,0:T(8,128)(2,1)}, bf16[512,1024]{1,0:T(8,128)(2,1)}) custom-call(bf16[512,128]{1,0:T(8,128)(2,1)} %q_ref.1, bf16[512,128]{1,0:T(8,128)(2,1)} %k_ref.1, bf16[512,1024]{1,0:T(8,128)(2,1)} %v_ref.1, f32[3,1024]{1,0:T(4,128)} %cw_ref.1, ...), custom_call_target="tpu_custom_call" | custom-call | tf_op jit(solution)/shard_map/pallas_call | solution.py:449
  65.5 4.8 %shard_map.156 = (bf16[512,1024]{1,0:T(8,128)(2,1)}, bf16[512,128]{1,0:T(8,128)(2,1)}, bf16[512,128]{1,0:T(8,128)(2,1)}, bf16[2,512,1024]{2,1,0:T(8,128)(2,1)}, bf16[512,1024]{1,0:T(8,128)(2,1)}) custom-call(bf16[512,1024]{1,0:T(8,128)(2,1)} %get-tuple-element.10.refs_0_, bf16[512,128]{1,0:T(8,128)(2,1)} %get-tuple-element.11.refs_1_, ...), custom_call_target="tpu_custom_call" | custom-call | tf_op jit(solution)/shard_map/pallas_call | solution.py:432

commit v2 on v1

--- a/solution.py
+++ b/solution.py
@@ -55,8 +55,9 @@
 
 def body(
     n, plane,
-    q_ref, k_ref, v_ref, cw_ref, gain_ref, wq_ref, wk_ref, ct_ref, e1_ref, e2_ref, col_ref, row_ref,
-    lo_ref, qg_ref, kg_ref, wg_ref, vg_ref,
+    q_ref, k_ref, v_ref, cw_ref, gain_ref, wq_hbm, wk_ref, ct_hbm, e1_ref, e2_ref, col_ref, row_ref,
+    lo_hbm, qg_ref, kg_ref, wg_hbm, vg_ref,
+    wq_ref, ct_ref, lo_ref, wg_ref, local,
     vrim, krim, kback_out, vback_out, kback, vback, vnext_out, vnext,
     cv, num, wo, klast, vw, ng, dq, dk, pkt, pqt, pq, pk, qa, qb, ka, kb,
     loc, buf_a, tot, buf_b, base, stage, buf_c,
@@ -76,6 +77,13 @@
             src_ref=src, dst_ref=dst, send_sem=ss, recv_sem=rs,
             device_id={"seq": to}, device_id_type=pl.DeviceIdType.MESH,
         )
+
+    wq_in = pltpu.make_async_copy(wq_hbm, wq_ref, local.at[0])
+    ct_in = pltpu.make_async_copy(ct_hbm, ct_ref, local.at[1])
+    lo_out = pltpu.make_async_copy(lo_ref, lo_hbm, local.at[2])
+    wg_out = pltpu.make_async_copy(wg_ref, wg_hbm, local.at[3])
+    wq_in.start()
+    ct_in.start()
 
     barrier = pltpu.get_barrier_semaphore()
 
@@ -301,6 +309,8 @@
         pq[h] = (one * two).astype(BF16)
         pqt[h] = turned(queries).astype(BF16)
 
+    wq_in.wait()
+    ct_in.wait()
     heads(0, 3, window)
     scan_b(0)
     heads(3, H, window)
@@ -325,6 +335,7 @@
 
     heads(0, H, normed)
     scan_a(1)
+    lo_out.start()
     dq[...] = jnp.zeros_like(dq)
     dk[...] = jnp.zeros_like(dk)
 
@@ -372,6 +383,7 @@
         vw[pl.ds(T - WIN, WIN), :] += vback[...].astype(F32)
 
     wg_ref[1, pl.ds(T - WIN, WIN), :] = klast[...].astype(BF16)
+    wg_out.start()
     scan_end(1)
 
     def far_value(h):
@@ -412,6 +424,8 @@
     pl.when(me > 0)(lambda: sent(next_copy()))
     scan_sent(0)
     scan_sent(1)
+    lo_out.wait()
+    wg_out.wait()
 
 
 def copies(*refs):
@@ -445,6 +459,7 @@
     R = H // plane * FP
     e1, e2, columns, rows = feature_tables()
     vmem = pl.BlockSpec(memory_space=pltpu.VMEM)
+    hbm = pl.BlockSpec(memory_space=pl.ANY)
     dma = pltpu.SemaphoreType.DMA
     outs = pl.pallas_call(
         partial(body, n, plane),
@@ -455,9 +470,14 @@
             jax.ShapeDtypeStruct((2, T, width), BF16),
             jax.ShapeDtypeStruct((T, width), BF16),
         ),
-        in_specs=[vmem] * 12,
-        out_specs=(vmem,) * 5,
+        in_specs=[vmem] * 5 + [hbm, vmem, hbm] + [vmem] * 4,
+        out_specs=(hbm, vmem, vmem, hbm, vmem),
         scratch_shapes=[
+            pltpu.VMEM((T, width), BF16),
+            pltpu.VMEM((T, width), BF16),
+            pltpu.VMEM((T, width), BF16),
+            pltpu.VMEM((2, T, width), BF16),
+            dma((4,)),
             pltpu.VMEM((RIM, width), BF16),
             pltpu.VMEM((WIN, width), BF16),
             pltpu.VMEM((WIN, width), BF16),

time: 70.5 us -> 69 us (0.979)
  Pallas kernels: 69.7 us -> 68.1 us
    pallas_call x1, Pallas kernels: 64.9 us -> 63.3 us  [shards(): pl.pallas_call(partial(body, n, plane), out_shape=(jax.ShapeDtypeStruct((...]
where the time goes in v2:
time: 69 us; the launch traced here: 68.8 us
  Pallas kernels  68.1 us (99%)
    pallas_call x1, Pallas kernels, shards(): pl.pallas_call(partial(body, n, plane), out_shape=(jax.ShapeDtypeStruct((...  63.3 us
    pallas_call x1, Pallas kernels, handed_on(): pl.pallas_call(copies, grid=(steps,), out_shape=tuple((jax.ShapeDtypeStru...  4.82 us

profile of v2, /device:TPU:1, one launch (start us, length us, event | category | flops | bytes accessed | tf_op | source)
XLA Modules:
  0.0 68.8 jit_solution(15064723270217309174)
XLA Ops:
  0.6 63.3 %shard_map.155 = (bf16[512,1024]{1,0:T(8,128)(2,1)}, bf16[512,128]{1,0:T(8,128)(2,1)}, bf16[512,128]{1,0:T(8,128)(2,1)}, bf16[2,512,1024]{2,1,0:T(8,128)(2,1)}, bf16[512,1024]{1,0:T(8,128)(2,1)}) custom-call(bf16[512,128]{1,0:T(8,128)(2,1)} %q_ref.1, bf16[512,128]{1,0:T(8,128)(2,1)} %k_ref.1, bf16[512,1024]{1,0:T(8,128)(2,1)} %v_ref.1, f32[3,1024]{1,0:T(4,128)} %cw_ref.1, ...), custom_call_target="tpu_custom_call" | custom-call | tf_op jit(solution)/shard_map/pallas_call | solution.py:464
  64.0 4.8 %shard_map.156 = (bf16[512,1024]{1,0:T(8,128)(2,1)}, bf16[512,128]{1,0:T(8,128)(2,1)}, bf16[512,128]{1,0:T(8,128)(2,1)}, bf16[2,512,1024]{2,1,0:T(8,128)(2,1)}, bf16[512,1024]{1,0:T(8,128)(2,1)}) custom-call(bf16[512,1024]{1,0:T(8,128)(2,1)} %get-tuple-element.10.refs_0_, bf16[512,128]{1,0:T(8,128)(2,1)} %get-tuple-element.11.refs_1_, ...), custom_call_target="tpu_custom_call" | custom-call | tf_op jit(solution)/shard_map/pallas_call | solution.py:446
